TPU v7x, 512 devices: a whole 4x8x8 slice. The times are simulated.
512 devices in a mesh: win: 16 (over x, z_hi, core), tile: 32 (over z_lo, y).
Axes of the slice: x: 4, y: 8, z: 8 (z_hi: 2, z_lo: 4; z = z_hi * 4 + z_lo), core: 2. Of those that a mesh axis runs over, the one named last changes fastest.
Arguments:
- increment: float32 [16, 128, 256, 512], P('win', None, 'tile'), may hold values from -6 to 6
- diffusivity: float32 [16, 256, 512], P('win', 'tile'), may hold values from 0.04 to 0.2
- wind: float32 [16, 128], P('win'), may hold values from -0.3 to 0.3
- vertical_cov: bfloat16 [128, 128], replicated, may hold values from -1 to 2, as said below
- row_cov: bfloat16 [256, 256], replicated, may hold values from -1 to 2, as said below
- column_cov: bfloat16 [512, 512], replicated, may hold values from -1 to 2, as said below
Outputs:
- covaried: float32 [16, 128, 256, 512], P('win', 'tile')
Inputs may be any that keep to these rules, and one draw needn't show every extreme that they name: `vertical_cov`: symmetric and positive definite. `row_cov`: symmetric and positive definite. `column_cov`: symmetric and positive definite.
All inputs are finite; a program needn't handle non-finite values.
Results may differ from a plain program's by a relative error of at most 0.0003.
Values sent between devices are 32-bit elements; how exact they have to be, the bound alone decides.
A program may use at most 64 MiB of HBM per device.

v0:
```python
import jax
import jax.numpy as jnp
from jax import lax
from jax.sharding import PartitionSpec as P

STEPS = 6


VMIX = 0.1


def with_halo(cells, sides, width):
    for axis, dim in sides:
        count = lax.axis_size(axis)
        ends = count - 1
        head = lax.slice_in_dim(cells, 0, width, axis=dim)
        tail = lax.slice_in_dim(cells, cells.shape[dim] - width, cells.shape[dim], axis=dim)
        cells = jnp.concatenate(
            [
                lax.ppermute(tail, axis, [(i, (i + 1) % count) for i in range(ends)]),
                cells,
                lax.ppermute(head, axis, [((i + 1) % count, i) for i in range(ends)]),
            ],
            axis=dim,
        )
    return cells


def passed_along(x, axis, by):
    size = lax.axis_size(axis)
    pairs = [(i, i + by) for i in range(size) if 0 <= i + by < size]
    return lax.ppermute(x, axis, pairs)


def tendency(center, north, south, kappa, wind_col):
    east = jnp.roll(center, -1, axis=2)
    west = jnp.roll(center, 1, axis=2)
    stacked = jnp.pad(center, ((1, 1), (0, 0), (0, 0)))
    upper = stacked[2:]
    lower = stacked[:-2]
    horiz = north + south + east + west - 4.0 * center
    vert = upper + lower - 2.0 * center
    return center + kappa[None] * horiz + VMIX * vert + wind_col * (0.5 * (south - north))


def advance(field, kappa, wind_col):
    rows = field.shape[1]
    depth = STEPS
    wide = with_halo(field, (("tile", 1),), depth)
    kappa_wide = with_halo(kappa, (("tile", 0),), depth)
    first = lax.axis_index("tile") * rows - depth
    places = first + jnp.arange(rows + 2 * depth, dtype=jnp.int32)
    inside = ((places >= 0) & (places < rows * lax.axis_size("tile"))).astype(jnp.float32)
    current = wide
    for step in range(STEPS):
        offset = step + 1
        count = current.shape[1] - 2
        fresh = tendency(
            current[:, 1:-1],
            current[:, 2:],
            current[:, :-2],
            kappa_wide[offset : offset + count],
            wind_col,
        )
        current = fresh * inside[offset : offset + count][None, :, None]
    return current


def fetch_next(field):
    return passed_along(field, "win", -1)


def body(increment, diffusivity, wind, vertical_cov, row_cov, column_cov):
    field = increment[0]
    kappa = diffusivity[0]
    wind_col = wind[0][:, None, None]
    evolved = advance(field, kappa, wind_col)
    following = fetch_next(field)
    defect = evolved - following
    levels, rows, width = defect.shape
    vert_mat = vertical_cov.astype(jnp.float32)
    col_mat = column_cov.astype(jnp.float32)
    row_mat = row_cov.astype(jnp.float32)
    mixed = jnp.dot(vert_mat, defect.reshape(levels, rows * width), precision=lax.Precision.HIGHEST)
    mixed = jnp.dot(mixed.reshape(levels * rows, width), col_mat, precision=lax.Precision.HIGHEST)
    mixed = mixed.reshape(levels, rows, width)
    covaried = jnp.einsum(
        "yk,zkx->zyx",
        row_mat,
        lax.all_to_all(mixed, "tile", split_axis=0, concat_axis=1, tiled=True),
        precision=lax.Precision.HIGHEST,
    )
    return covaried[None]


def solution(mesh):
    in_specs = (P("win", None, "tile", None), P("win", "tile", None), P("win", None), P(), P(), P())
    out_specs = P("win", "tile", None, None)
    return jax.shard_map(body, mesh=mesh, in_specs=in_specs, out_specs=out_specs, check_vma=False)
```

profile of v0, /device:TPU:1, one launch (start us, length us, event | category | flops | bytes accessed | tf_op | source)
XLA Modules:
  0.0 176.3 jit_solution(7756594273389456896)
XLA Ops:
  0.0 2.0 %copy.19 = f32[1,128,8,512]{1,3,2,0:T(8,128)S(1)} copy(f32[1,128,8,512]{3,2,1,0:T(8,128)} %param.6) | data formatting | bytes 4194304 | tf_op args[0]
  2.1 2.0 %fusion.84 = (f32[128,6,512]{0,2,1:T(8,128)}, f32[128,6,512]{0,2,1:T(8,128)}) fusion(f32[128,8,512]{0,2,1:T(8,128)S(1)} %bitcast.33), kind=kLoop, calls=%fused_computation.109 | loop fusion | bytes 6291456 | tf_op jit(solution)/shard_map/slice | solution.py:17
  4.1 3.1 %copy.20 = f32[128,6,512]{2,0,1:T(8,128)} copy(f32[128,6,512]{0,2,1:T(8,128)} %get-tuple-element.27) | data formatting | bytes 3145728 | tf_op jit(solution)/shard_map/slice | solution.py:17
  7.1 5.2 %collective-permute-start = (f32[128,6,512]{2,0,1:T(8,128)}, f32[128,6,512]{2,0,1:T(8,128)}, u32[]{:S(2)}, u32[]{:S(2)}) collective-permute-start(f32[128,6,512]{2,0,1:T(8,128)} %copy.20), channel_id=1, source_target_pairs={{0,1},{1,2},{2,3},{3,4},{4,5},{5,6},{6,7},{7,8},{8,9},{9,10},{10,1... | collective-permute-start | bytes 4718600 | tf_op jit(solution)/shard_map/ppermute | solution.py:20
  12.3 3.0 %copy.21 = f32[128,6,512]{2,0,1:T(8,128)} copy(f32[128,6,512]{0,2,1:T(8,128)} %get-tuple-element.28) | data formatting | bytes 3145728 | tf_op jit(solution)/shard_map/slice | solution.py:16
  16.6 6.0 %collective-permute-start.4 = (f32[128,8,512]{0,2,1:T(8,128)S(1)}, f32[128,8,512]{0,2,1:T(8,128)}, u32[]{:S(2)}, u32[]{:S(2)}) collective-permute-start(f32[128,8,512]{0,2,1:T(8,128)S(1)} %bitcast.34), channel_id=1, source_target_pairs={{32,0},{64,32},{96,64},{128,96},{160,128},{192,160},{224,192},{256... | collective-permute-start | bytes 6291464 | tf_op jit(solution)/shard_map/ppermute | solution.py:32
  22.7 4.3 %collective-permute-start.2 = (f32[6,512]{1,0:T(8,128)S(1)}, f32[6,512]{1,0:T(8,128)S(1)}, u32[]{:S(2)}, u32[]{:S(2)}) collective-permute-start(f32[6,512]{1,0:T(8,128)S(1)} %get-tuple-element.29), channel_id=1, source_target_pairs={{0,1},{1,2},{2,3},{3,4},{4,5},{5,6},{6,7},{7,8},{8,9},{9,10},{10,1... | collective-permute-start | bytes 36872 | tf_op jit(solution)/shard_map/ppermute | solution.py:20
  28.7 12.8 %collective-permute-done.2 = f32[6,512]{1,0:T(8,128)S(1)} collective-permute-done((f32[6,512]{1,0:T(8,128)S(1)}, f32[6,512]{1,0:T(8,128)S(1)}, u32[]{:S(2)}, u32[]{:S(2)}) %collective-permute-start.2) | collective-permute-done | bytes 12320 | tf_op jit(solution)/shard_map/ppermute | solution.py:20
  41.5 8.1 %collective-permute-done.3 = f32[6,512]{1,0:T(8,128)S(1)} collective-permute-done((f32[6,512]{1,0:T(8,128)S(1)}, f32[6,512]{1,0:T(8,128)S(1)}, u32[]{:S(2)}, u32[]{:S(2)}) %collective-permute-start.3) | collective-permute-done | bytes 12320 | tf_op jit(solution)/shard_map/ppermute | solution.py:22
  49.7 3.1 %copy.22 = f32[128,6,512]{0,2,1:T(8,128)} copy(f32[128,6,512]{2,0,1:T(8,128)} %collective-permute-done) | data formatting | bytes 3145728 | tf_op jit(solution)/shard_map/ppermute | solution.py:20
  52.8 3.0 %copy.23 = f32[128,6,512]{0,2,1:T(8,128)} copy(f32[128,6,512]{2,0,1:T(8,128)} %collective-permute-done.1) | data formatting | bytes 3145728 | tf_op jit(solution)/shard_map/ppermute | solution.py:22
  55.9 2.2 %pad_maximum_fusion = f32[128,20,512]{0,2,1:T(8,128)S(1)} fusion(f32[128,6,512]{0,2,1:T(8,128)} %copy.23, f32[128,8,512]{0,2,1:T(8,128)S(1)} %bitcast.35, f32[128,6,512]{0,2,1:T(8,128)} %copy.22), kind=kLoop, calls=%fused_computation.10 | loop fusion | flops 2621440 | bytes 10485760 | tf_op jit(solution)/shard_map/concatenate | solution.py:18
  58.1 4.6 %fusion.73 = (f32[128,18,511]{0,2,1:T(8,128)}, f32[128,18,511]{0,2,1:T(8,128)}) fusion(f32[128,20,512]{0,2,1:T(8,128)S(1)} %pad_maximum_fusion), kind=kLoop, calls=%fused_computation.98 | loop fusion | bytes 18837504 | tf_op jit(solution)/shard_map/jit(_roll_static)/slice | solution.py:37
  63.0 2.0 %copy-done.1 = f32[128,18,511]{0,2,1:T(8,128)S(1)} copy-done((f32[128,18,511]{0,2,1:T(8,128)S(1)}, f32[128,18,511]{0,2,1:T(8,128)}, u32[]{:S(2)}) %copy-start.1) | copy-done | bytes 4709400
  66.5 8.9 %fusion.5 = f32[128,18,512]{0,2,1:T(8,128)S(1)} fusion(f32[128,18,512]{0,2,1:T(8,128)S(1)} %slice.334, f32[128,6,512]{0,2,1:T(8,128)} %copy.23, f32[128,8,512]{0,2,1:T(8,128)S(1)} %bitcast.36, f32[128,6,512]{0,2,1:T(8,128)} %copy.22, f32[128,18,511]{0,2,1:T(8,128)S(1)} %copy-done.2, f32[128,18,511]{0,2,1:T(8,128)S(1)} %copy-done.1, ...), kind=kLoop, calls=%fused_computation.18 | loop fusion | flops 25952256 | bytes 33573448 | tf_op jit(solution)/shard_map/mul | solution.py:65
  76.5 4.0 %fusion.18 = f32[128,16,512]{0,2,1:T(8,128)S(1)} fusion(f32[128,16,512]{0,2,1:T(8,128)S(1)} %slice.340, f32[128,16,1]{0,2,1:T(1,128)S(1)} %get-tuple-element.8, f32[128,16,511]{0,2,1:T(8,128)S(1)} %get-tuple-element.10, f32[128,16,511]{0,2,1:T(8,128)S(1)} %get-tuple-element.9, f32[128,16,1]{0,2,1:T(1,128)S(1)} %get-tuple-element.7, ...), kind=kLoop, calls=%fused_computation.35 | loop fusion | flops 18874368 | bytes 25199168 | tf_op jit(solution)/shard_map/mul | solution.py:65
  81.5 4.0 %fusion.28 = f32[128,14,512]{0,2,1:T(8,128)S(1)} fusion(f32[128,14,512]{0,2,1:T(8,128)S(1)} %slice.348, f32[128,14,1]{0,2,1:T(1,128)S(1)} %get-tuple-element.12, f32[128,14,511]{0,2,1:T(8,128)S(1)} %get-tuple-element.14, f32[128,14,511]{0,2,1:T(8,128)S(1)} %get-tuple-element.13, f32[128,14,1]{0,2,1:T(1,128)S(1)} %get-tuple-element.11, ...), kind=kLoop, calls=%fused_computation.46 | loop fusion | flops 16515072 | bytes 22049336 | tf_op jit(solution)/shard_map/mul | solution.py:65
  86.3 3.0 %fusion.38 = f32[128,12,512]{0,2,1:T(8,128)S(1)} fusion(f32[128,12,512]{0,2,1:T(8,128)S(1)} %slice.356, f32[128,12,1]{0,2,1:T(1,128)S(1)} %get-tuple-element.16, f32[128,12,511]{0,2,1:T(8,128)S(1)} %get-tuple-element.18, f32[128,12,511]{0,2,1:T(8,128)S(1)} %get-tuple-element.17, f32[128,12,1]{0,2,1:T(1,128)S(1)} %get-tuple-element.15, ...), kind=kLoop, calls=%fused_computation.57 | loop fusion | flops 14155776 | bytes 18899504 | tf_op jit(solution)/shard_map/mul | solution.py:65
  90.0 3.1 %fusion.48 = f32[128,10,512]{0,2,1:T(8,128)S(1)} fusion(f32[128,10,512]{0,2,1:T(8,128)S(1)} %slice.364, f32[128,10,1]{0,2,1:T(1,128)S(1)} %get-tuple-element.20, f32[128,10,511]{0,2,1:T(8,128)S(1)} %get-tuple-element.22, f32[128,10,511]{0,2,1:T(8,128)S(1)} %get-tuple-element.21, f32[128,10,1]{0,2,1:T(1,128)S(1)} %get-tuple-element.19, ...), kind=kLoop, calls=%fused_computation.68 | loop fusion | flops 11796480 | bytes 15749672 | tf_op jit(solution)/shard_map/mul | solution.py:65
  93.6 3.3 %fusion.59 = f32[128,8,512]{0,2,1:T(8,128)S(1)} fusion(f32[128,8,512]{0,2,1:T(8,128)} %collective-permute-done.4, f32[128,8,512]{0,2,1:T(8,128)S(1)} %slice.372, f32[128,8,1]{0,2,1:T(1,128)S(1)} %get-tuple-element.24, f32[128,8,511]{0,2,1:T(8,128)S(1)} %get-tuple-element.26, f32[128,8,511]{0,2,1:T(8,128)S(1)} %get-tuple-element.25, ...), kind=kLoop, calls=%fused_computation.80 | loop fusion | flops 9961472 | bytes 14696992 | tf_op jit(solution)/shard_map/sub | solution.py:79
  98.0 2.0 %copy.29 = f32[128,8,512]{2,1,0:T(8,128)} copy(f32[128,8,512]{0,2,1:T(8,128)S(1)} %bitcast.37) | data formatting | bytes 4194304 | tf_op jit(solution)/shard_map/dot_general | solution.py:85
  99.9 3.4 %fusion.70 = f32[128,8,512]{2,1,0:T(8,128)S(1)} fusion(f32[128,8,512]{2,1,0:T(8,128)} %copy.29, bf16[512,512]{1,0:T(8,128)(2,1)S(1)} %copy-done), kind=kOutput, calls=%fused_computation.90 | convolution fusion | flops 3221225472 | bytes 4718592 | tf_op jit(solution)/shard_map/dot_general | solution.py:85
  103.3 69.3 %all_to_all.18 = f32[128,8,512]{2,1,0:T(8,128)S(1)} all-to-all(f32[128,8,512]{2,1,0:T(8,128)S(1)} %fusion.70), channel_id=1, replica_groups=mesh['win'=16,'tile'=32] {'tile'}, dimensions={0} | all-to-all | bytes 4194304 | tf_op jit(solution)/shard_map/all_to_all | solution.py:90
  172.6 1.9 %fusion.67 = f32[1,4,256,512]{2,3,1,0:T(8,128)S(1)} fusion(f32[4,32,8,512]{3,2,0,1:T(8,128)S(1)} %bitcast.38, bf16[256,256]{1,0:T(8,128)(2,1)S(1)} %copy-done.4), kind=kOutput, calls=%fused_computation.89 | convolution fusion | flops 1610612736 | bytes 4325376 | tf_op jit(solution)/shard_map/yk,zkx->zyx/dot_general | solution.py:87
  (51 shorter events, 11.8 us)
Async XLA Ops:
  0.0 99.9 %copy-start = (bf16[512,512]{1,0:T(8,128)(2,1)S(1)}, bf16[512,512]{1,0:T(8,128)(2,1)}, u32[]{:S(2)}) copy-start(bf16[512,512]{1,0:T(8,128)(2,1)} %param.11) | copy-start | bytes 1572868
  4.0 18.6 %copy-start.3 = (f32[1,8,512]{2,1,0:T(8,128)S(1)}, f32[1,8,512]{2,1,0:T(8,128)}, u32[]{:S(2)}) copy-start(f32[1,8,512]{2,1,0:T(8,128)} %param.7) | copy-start | bytes 49156
  4.0 24.2 %copy-start.6 = (f32[1,128]{1,0:T(1,128)S(1)}, f32[1,128]{1,0:T(1,128)}, u32[]{:S(2)}) copy-start(f32[1,128]{1,0:T(1,128)} %param.8) | copy-start | bytes 1540
  7.1 42.6 %collective-permute-start = (f32[128,6,512]{2,0,1:T(8,128)}, f32[128,6,512]{2,0,1:T(8,128)}, u32[]{:S(2)}, u32[]{:S(2)}) collective-permute-start(f32[128,6,512]{2,0,1:T(8,128)} %copy.20), channel_id=1, source_target_pairs={{0,1},{1,2},{2,3},{3,4},{4,5},{5,6},{6,7},{7,8},{8,9},{9,10},{10,1... | collective-permute-start | bytes 4718600 | tf_op jit(solution)/shard_map/ppermute | solution.py:20
  15.3 37.5 %collective-permute-start.1 = (f32[128,6,512]{2,0,1:T(8,128)}, f32[128,6,512]{2,0,1:T(8,128)}, u32[]{:S(2)}, u32[]{:S(2)}) collective-permute-start(f32[128,6,512]{2,0,1:T(8,128)} %copy.21), channel_id=1, source_target_pairs={{1,0},{2,1},{3,2},{4,3},{5,4},{6,5},{7,6},{8,7},{9,8},{10,9},{11,1... | collective-permute-start | bytes 4718600 | tf_op jit(solution)/shard_map/ppermute | solution.py:22
  16.6 77.0 %collective-permute-start.4 = (f32[128,8,512]{0,2,1:T(8,128)S(1)}, f32[128,8,512]{0,2,1:T(8,128)}, u32[]{:S(2)}, u32[]{:S(2)}) collective-permute-start(f32[128,8,512]{0,2,1:T(8,128)S(1)} %bitcast.34), channel_id=1, source_target_pairs={{32,0},{64,32},{96,64},{128,96},{160,128},{192,160},{224,192},{256... | collective-permute-start | bytes 6291464 | tf_op jit(solution)/shard_map/ppermute | solution.py:32
  22.7 18.8 %collective-permute-start.2 = (f32[6,512]{1,0:T(8,128)S(1)}, f32[6,512]{1,0:T(8,128)S(1)}, u32[]{:S(2)}, u32[]{:S(2)}) collective-permute-start(f32[6,512]{1,0:T(8,128)S(1)} %get-tuple-element.29), channel_id=1, source_target_pairs={{0,1},{1,2},{2,3},{3,4},{4,5},{5,6},{6,7},{7,8},{8,9},{9,10},{10,1... | collective-permute-start | bytes 36872 | tf_op jit(solution)/shard_map/ppermute | solution.py:20
  27.0 22.7 %collective-permute-start.3 = (f32[6,512]{1,0:T(8,128)S(1)}, f32[6,512]{1,0:T(8,128)S(1)}, u32[]{:S(2)}, u32[]{:S(2)}) collective-permute-start(f32[6,512]{1,0:T(8,128)S(1)} %get-tuple-element.30), channel_id=1, source_target_pairs={{1,0},{2,1},{3,2},{4,3},{5,4},{6,5},{7,6},{8,7},{9,8},{10,9},{11,1... | collective-permute-start | bytes 36872 | tf_op jit(solution)/shard_map/ppermute | solution.py:22
  62.7 2.3 %copy-start.1 = (f32[128,18,511]{0,2,1:T(8,128)S(1)}, f32[128,18,511]{0,2,1:T(8,128)}, u32[]{:S(2)}) copy-start(f32[128,18,511]{0,2,1:T(8,128)} %get-tuple-element.5) | copy-start | bytes 14128132
  62.7 3.8 %copy-start.2 = (f32[128,18,511]{0,2,1:T(8,128)S(1)}, f32[128,18,511]{0,2,1:T(8,128)}, u32[]{:S(2)}) copy-start(f32[128,18,511]{0,2,1:T(8,128)} %get-tuple-element.6) | copy-start | bytes 14128132
  93.6 3.3 %copy-start.5 = (bf16[128,128]{1,0:T(8,128)(2,1)S(1)}, bf16[128,128]{1,0:T(8,128)(2,1)}, u32[]{:S(2)}) copy-start(bf16[128,128]{1,0:T(8,128)(2,1)} %param.9) | copy-start | bytes 98308
  103.3 69.3 %copy-start.4 = (bf16[256,256]{1,0:T(8,128)(2,1)S(1)}, bf16[256,256]{1,0:T(8,128)(2,1)}, u32[]{:S(2)}) copy-start(bf16[256,256]{1,0:T(8,128)(2,1)} %param.10) | copy-start | bytes 393220
where the time goes:
time: 177 us; the launch traced here: 176 us
  blocking collectives  69.3 us (39%)
  local copies, waits for them, and re-layouts  33 us (19%)
  other arithmetic  28.4 us (16%)
  waiting for transfers between devices  20.9 us (12%)
  starting transfers between devices  18.1 us (10%)
  matrix products  6.32 us (4%)
    all_to_all x1, blocking collectives, body(): lax.all_to_all(mixed, 'tile', split_axis=0, concat_axis=1, tiled=True)  69.3 us
    mul x5, other arithmetic, advance(): current = fresh * inside[offset:offset + count][None, :, None]  22.9 us
    ppermute x2, waiting for transfers between devices, with_halo(): lax.ppermute(tail, axis, [(i, (i + 1) % count) for i in range(ends)])  12.8 us
    ppermute x2, starting transfers between devices, with_halo(): lax.ppermute(tail, axis, [(i, (i + 1) % count) for i in range(ends)])  9.45 us
    ppermute x2, waiting for transfers between devices, with_halo(): lax.ppermute(head, axis, [((i + 1) % count, i) for i in range(ends)])  8.11 us
    slice x11, local copies, waits for them, and re-layouts, tendency(): west = jnp.roll(center, 1, axis=2)  7.58 us
    ppermute x1, starting transfers between devices, passed_along(): return lax.ppermute(x, axis, pairs)  6.05 us
    unnamed x15, local copies, waits for them, and re-layouts  5.52 us
  transfers between devices with their start and end apart: 5, of which 2 were waited for; matrix products, arithmetic and copies ran while one was open for 25% of the time, Pallas kernels for 0%

commit v1 on v0

v1 whole, which is shorter than its diff:
```python
import functools

import jax
import jax.numpy as jnp
from jax import lax
from jax.experimental import pallas as pl
from jax.experimental.pallas import tpu as pltpu
from jax.sharding import PartitionSpec as P

STEPS = 6
L, ROWS, NX = 128, 8, 512
NY = 256
C = NX // 128
H = STEPS
R20 = ROWS + 2 * H
PAD = 8
MESH = pl.DeviceIdType.MESH
F32, BF16 = jnp.float32, jnp.bfloat16


def split2(v):
    hi = v.astype(BF16)
    lo = (v - hi.astype(F32)).astype(BF16)
    return hi, lo


def kernel(
    inc_ref, dif_ref, wind_ref, vert_ref, row_ref, col_ref, out_ref,
    inb, x, xb, kap, wbuf, fb, mf, me, ze, zf, g, rb, zb, ob,
    in_sem, dif_sem, out_sem, loc_e, loc_y,
    halo_s, halo_r, kap_s, kap_r, raw_s, raw_r, f_s, f_r, e_s, e_r, y_s, y_r, go_sem,
):
    w = lax.axis_index("win")
    tile = lax.axis_index("tile")
    core = lax.rem(w, 2)
    a = tile // 8
    yy = lax.rem(tile, 8)
    even, odd = core == 0, core == 1
    has_prev, has_next = tile > 0, tile < 31
    sends_f = jnp.logical_and(even, w > 0)
    gets_f = jnp.logical_and(odd, w < 15)

    in_cps = [
        pltpu.make_async_copy(inc_ref.at[:, pl.ds(128 * c, 128)], inb.at[c], in_sem.at[c])
        for c in range(C)
    ]
    for cp in in_cps:
        cp.start()
    dif_cps = [
        pltpu.make_async_copy(dif_ref.at[:, pl.ds(128 * c, 128)], kap.at[1, c], dif_sem.at[c])
        for c in range(C)
    ]
    for cp in dif_cps:
        cp.start()

    bar = pltpu.get_barrier_semaphore()

    def greet(dev):
        pl.semaphore_signal(bar, inc=1, device_id=dev, device_id_type=MESH)

    pl.when(has_prev)(lambda: greet((w, tile - 1)))
    pl.when(has_next)(lambda: greet((w, tile + 1)))
    for d in range(1, 4):
        greet((w, lax.rem(a + d, 4) * 8 + yy))
    for d in range(1, 8):
        greet((w, a * 8 + lax.rem(yy + d, 8)))
    sib = w + 1 - 2 * core
    greet((sib, tile))

    @pl.when(gets_f)
    def _():
        for b in range(4):
            greet((w + 1, b * 8 + yy))

    zero8 = jnp.zeros((8, 128), F32)

    @pl.loop(0, R20)
    def _(r):
        for f in (x, xb):
            for c in range(C):
                f[c, r, 0:8, :] = zero8
                f[c, r, PAD + L : PAD + L + 8, :] = zero8

    def clear_rows(first):
        @pl.loop(first, first + H)
        def _(r):
            for f in (x, xb):
                for c in range(C):
                    f[c, r, PAD : PAD + L, :] = jnp.zeros((L, 128), F32)

    pl.when(jnp.logical_not(has_prev))(lambda: clear_rows(0))
    pl.when(jnp.logical_not(has_next))(lambda: clear_rows(H + ROWS))

    wbuf[...] = jnp.transpose(jnp.broadcast_to(wind_ref[...] * 5.0, (128, 128)))
    vert = vert_ref[...]
    vv = jnp.concatenate([vert, vert], axis=1)

    for cp in in_cps:
        cp.wait()
    for c in range(C):
        for y in range(ROWS):
            x[c, H + y, PAD : PAD + L, :] = inb[c, pl.ds(y, L, stride=8), :]
    for cp in dif_cps:
        cp.wait()

    peers = 11 + has_prev.astype(jnp.int32) + has_next.astype(jnp.int32) + jnp.where(sends_f, 4, 0)
    pl.semaphore_wait(bar, peers)

    raw = pltpu.make_async_remote_copy(
        src_ref=inb, dst_ref=fb, send_sem=raw_s, recv_sem=raw_r,
        device_id=(sib, tile), device_id_type=MESH,
    )

    @pl.when(odd)
    def _():
        raw.start()
        pl.semaphore_wait(go_sem, 1)

    def remote(src, dst, ss, rs, dev):
        return pltpu.make_async_remote_copy(
            src_ref=src, dst_ref=dst, send_sem=ss, recv_sem=rs, device_id=dev, device_id_type=MESH
        )

    zs = pl.ds(PAD, L)
    up = remote(
        x.at[:, pl.ds(H, H), zs], x.at[:, pl.ds(H + ROWS, H), zs],
        halo_s.at[0], halo_r.at[0], (w, tile - 1),
    )
    down = remote(
        x.at[:, pl.ds(ROWS, H), zs], x.at[:, pl.ds(0, H), zs],
        halo_s.at[1], halo_r.at[1], (w, tile + 1),
    )
    kup = remote(kap.at[1], kap.at[2], kap_s.at[0], kap_r.at[0], (w, tile - 1))
    kdown = remote(kap.at[1], kap.at[0], kap_s.at[1], kap_r.at[1], (w, tile + 1))

    @pl.when(has_prev)
    def _():
        kup.start()
        up.start()

    @pl.when(has_next)
    def _():
        kdown.start()
        down.start()

    def level_mix(fields, c, dst, scale=None, base=None):
        @pl.loop(0, ROWS // 2)
        def _(pair):
            parts = []
            for i in range(2):
                y = 2 * pair + i
                v = fields[c, H + y, PAD : PAD + L, :]
                if scale is not None:
                    v = v * scale - base[c, pl.ds(y, L, stride=8), :]
                parts.append(v)
            hi, lo = split2(jnp.concatenate(parts, axis=1))
            mixed = jnp.dot(vv, jnp.concatenate([hi, lo], axis=0), preferred_element_type=F32)
            for i in range(2):
                for b in range(4):
                    dst[b, c, 2 * pair + i] = mixed[32 * b : 32 * b + 32, 128 * i : 128 * i + 128]

    f_cps = [
        remote(
            mf.at[lax.rem(a + d, 4)], zf.at[a], f_s.at[d], f_r.at[d],
            (lax.rem(w + 15, 16), lax.rem(a + d, 4) * 8 + yy),
        )
        for d in range(4)
    ]

    @pl.when(sends_f)
    def _():
        for c in range(C):
            level_mix(x, c, mf)
        for cp in f_cps:
            cp.start()

    @pl.when(jnp.logical_not(gets_f))
    def _():
        @pl.loop(0, 4)
        def _(i):
            for c in range(C):
                zf[i, c] = jnp.zeros((ROWS, 32, 128), F32)

    @pl.when(odd)
    def _():
        @pl.loop(0, C)
        def _(c):
            fb[c] = jnp.zeros((L * ROWS, 128), F32)

    @pl.when(has_prev)
    def _():
        kup.wait_send()
        kdown.wait_recv()
        down.wait_recv()

    @pl.when(has_next)
    def _():
        kdown.wait_send()
        kup.wait_recv()
        up.wait_recv()

    @pl.when(even)
    def _():
        pl.semaphore_signal(go_sem, inc=1, device_id=(sib, tile), device_id_type=MESH)

    pl.when(has_prev)(lambda: up.wait_send())
    pl.when(has_next)(lambda: down.wait_send())

    lane = lax.broadcasted_iota(jnp.int32, (8, 128), 1)
    first_lane, last_lane = lane == 0, lane == 127
    low = jnp.where(has_prev, 0, H)
    high = jnp.where(has_next, R20, H + ROWS)

    def step(s, src, dst):
        @pl.loop(jnp.maximum(low, s + 1), jnp.minimum(high, R20 - 1 - s))
        def _(r):
            kr = r + 2
            kt, ks = kr // 8, lax.rem(kr, 8)
            kb = [jnp.broadcast_to(kap[kt, c, pl.ds(ks, 1), :] * 10.0, (8, 128)) for c in range(C)]
            ab = [8.0 - 4.0 * k for k in kb]
            for zt in range(L // 8):
                z0 = PAD + 8 * zt
                wz = wbuf[8 * zt : 8 * zt + 8, :]
                cs = [src[c, r, z0 : z0 + 8, :] for c in range(C)]
                rr = [pltpu.roll(v, 1, 1) for v in cs]
                rl = [pltpu.roll(v, 127, 1) for v in cs]
                for c in range(C):
                    west = jnp.where(first_lane, rr[(c + C - 1) % C], rr[c])
                    east = jnp.where(last_lane, rl[(c + 1) % C], rl[c])
                    north = src[c, r + 1, z0 : z0 + 8, :]
                    south = src[c, r - 1, z0 : z0 + 8, :]
                    vert_sum = src[c, r, z0 + 1 : z0 + 9, :] + src[c, r, z0 - 1 : z0 + 7, :]
                    dst[c, r, z0 : z0 + 8, :] = (
                        (vert_sum + ab[c] * cs[c])
                        + kb[c] * ((north + south) + (east + west))
                        + wz * (south - north)
                    )

    @pl.loop(0, STEPS // 2)
    def _(h):
        step(2 * h, x, xb)
        step(2 * h + 1, xb, x)

    pl.when(even)(lambda: raw.wait_recv())

    e_cps = [[None] * 4 for _ in range(C)]
    e_loc = []
    for c in range(C):
        level_mix(x, c, me, 1e-6, fb)
        for d in (1, 3, 2):
            b = lax.rem(a + d, 4)
            cp = remote(me.at[b, c], ze.at[a, c], e_s.at[c, d], e_r.at[c, d], (w, b * 8 + yy))
            cp.start()
            e_cps[c][d] = cp
        cp = pltpu.make_async_copy(me.at[a, c], ze.at[a, c], loc_e.at[c])
        cp.start()
        e_loc.append(cp)

    @pl.when(gets_f)
    def _():
        for cp in f_cps:
            cp.wait_recv()

    y_cps = [[None] * 8 for _ in range(C)]
    y_loc = []
    for c in range(C):
        for d in (1, 3, 2):
            e_cps[c][d].wait_recv()
        e_loc[c].wait()

        @pl.loop(0, 4)
        def _(i, c=c):
            for y in range(ROWS):
                for t in range(4):
                    v = ze[i, c, y, 8 * t : 8 * t + 8, :] - zf[i, c, y, 8 * t : 8 * t + 8, :]
                    at = pl.ds(pl.multiple_of(i * 32, 32) + 4 * y, 4)
                    g[c, 2 * t, at, :] = v[0:4]
                    g[c, 2 * t + 1, at, :] = v[4:8]

        for d in (1, 7, 2, 6, 3, 5, 4):
            t = lax.rem(yy + d, 8)
            cp = remote(g.at[c, t], rb.at[yy, c], y_s.at[c, d], y_r.at[c, d], (w, a * 8 + t))
            cp.start()
            y_cps[c][d] = cp
        cp = pltpu.make_async_copy(g.at[c, yy], rb.at[yy, c], loc_y.at[c])
        cp.start()
        y_loc.append(cp)

    for d in (0, 1, 7, 2, 6, 3, 5, 4):
        src = lax.rem(yy + 8 - d, 8)
        for c in range(C):
            if d == 0:
                y_loc[c].wait()
            else:
                y_cps[c][d].wait_recv()
        total = None
        for c in range(C):
            v = jnp.concatenate([rb[src, c, pl.ds(z, 32, stride=4), :] for z in range(4)], axis=0)
            hi, lo = split2(v)
            cm = col_ref[128 * c : 128 * c + 128, :]
            part = jnp.dot(hi, cm, preferred_element_type=F32) + jnp.dot(lo, cm, preferred_element_type=F32)
            total = part if total is None else total + part
        for z in range(4):
            for i in range(4):
                k = z * 32 + i * 8
                zb[z, pl.ds(pl.multiple_of(64 * i + 8 * src, 8), 8), :] = total[k : k + 8]

    outs = []
    for z in range(4):
        hi, lo = split2(zb[z])
        rm = row_ref[...]
        ob[z] = jnp.dot(rm, hi, preferred_element_type=F32) + jnp.dot(rm, lo, preferred_element_type=F32)
        cp = pltpu.make_async_copy(ob.at[z], out_ref.at[z], out_sem.at[z])
        cp.start()
        outs.append(cp)

    pl.when(odd)(lambda: raw.wait_send())

    @pl.when(sends_f)
    def _():
        for cp in f_cps:
            cp.wait_send()

    for c in range(C):
        for d in range(1, 4):
            e_cps[c][d].wait_send()
        for d in range(1, 8):
            y_cps[c][d].wait_send()
    for cp in outs:
        cp.wait()


def body(increment, diffusivity, wind, vertical_cov, row_cov, column_cov):
    dma = pltpu.SemaphoreType.DMA
    anyspec = pl.BlockSpec(memory_space=pl.ANY)
    vm = pl.BlockSpec(memory_space=pltpu.VMEM)
    out = pl.pallas_call(
        kernel,
        out_shape=jax.ShapeDtypeStruct((4, NY, NX), F32),
        in_specs=[anyspec, anyspec, vm, vm, vm, vm],
        out_specs=anyspec,
        scratch_shapes=[
            pltpu.VMEM((C, L * ROWS, 128), F32),
            pltpu.VMEM((C, R20, L + 2 * PAD, 128), F32),
            pltpu.VMEM((C, R20, L + 2 * PAD, 128), F32),
            pltpu.VMEM((3, C, ROWS, 128), F32),
            pltpu.VMEM((L, 128), F32),
            pltpu.VMEM((C, L * ROWS, 128), F32),
            pltpu.VMEM((4, C, ROWS, 32, 128), F32),
            pltpu.VMEM((4, C, ROWS, 32, 128), F32),
            pltpu.VMEM((4, C, ROWS, 32, 128), F32),
            pltpu.VMEM((4, C, ROWS, 32, 128), F32),
            pltpu.VMEM((C, 8, 128, 128), F32),
            pltpu.VMEM((8, C, 128, 128), F32),
            pltpu.VMEM((4, NY, NX), F32),
            pltpu.VMEM((4, NY, NX), F32),
            dma((C,)), dma((C,)), dma((4,)), dma((C,)), dma((C,)),
            dma((2,)), dma((2,)), dma((2,)), dma((2,)), dma, dma,
            dma((4,)), dma((4,)), dma((C, 4)), dma((C, 4)), dma((C, 8)), dma((C, 8)),
            pltpu.SemaphoreType.REGULAR,
        ],
        compiler_params=pltpu.CompilerParams(
            collective_id=0, has_side_effects=True, vmem_limit_bytes=56 * 1024 * 1024
        ),
    )(
        increment.reshape(L * ROWS, NX), diffusivity[0], wind, vertical_cov, row_cov, column_cov
    )
    return out[None]


def solution(mesh):
    in_specs = (P("win", None, "tile", None), P("win", "tile", None), P("win", None), P(), P(), P())
    out_specs = P("win", "tile", None, None)
    return jax.shard_map(body, mesh=mesh, in_specs=in_specs, out_specs=out_specs, check_vma=False)
```

time: 177 us -> 143 us (0.81)
  the two profiles are of different devices: /device:TPU:1 before, /device:TPU:399 now
where the time goes in v1:
time: 143 us; the launch traced here: 142 us
  Pallas kernels  139 us (97%)
  local copies, waits for them, and re-layouts  3.08 us (2%)
    pallas_call x1, Pallas kernels, body(): pl.pallas_call(kernel, out_shape=jax.ShapeDtypeStruct((4, NY, NX), F32),...  139 us
    unnamed x1, local copies, waits for them, and re-layouts  3.08 us

profile of v1, /device:TPU:399, one launch (start us, length us, event | category | flops | bytes accessed | tf_op | source)
XLA Modules:
  0.0 142.3 jit_solution(6747815435224522706)
XLA Ops:
  0.0 139.3 %shard_map.64 = f32[4,256,512]{2,1,0:T(8,128)} custom-call(f32[1024,512]{1,0:T(8,128)} %bitcast.4, f32[8,512]{1,0:T(8,128)} %bitcast.5, f32[1,128]{1,0:T(1,128)} %wind_ref.1, bf16[128,128]{1,0:T(8,128)(2,1)} %vert_ref.1, bf16[256,256]{1,0:T(8,128)(2,1)} %row_ref.1, bf16[512,512]{1,0:T(8,128)(2,1)} %col_ref.1), custom_call_target="tpu_custom_call" | custom-call | tf_op jit(solution)/shard_map/pallas_call | solution.py:337
  139.3 3.1 %copy.8 = f32[1,4,256,512]{3,2,1,0:T(8,128)} copy(f32[1,4,256,512]{3,2,1,0:T(8,128)} %bitcast.3) | data formatting | bytes 4194304

commit v2 on v1

--- a/solution.py
+++ b/solution.py
@@ -14,6 +14,8 @@
 H = STEPS
 R20 = ROWS + 2 * H
 PAD = 8
+AHEAD = 2
+ORDER = [dz * 8 + dy for dy in (4, 3, 5, 2, 6, 1, 7, 0) for dz in (2, 1, 3, 0) if dz or dy]
 MESH = pl.DeviceIdType.MESH
 F32, BF16 = jnp.float32, jnp.bfloat16
 
@@ -26,9 +28,9 @@
 
 def kernel(
     inc_ref, dif_ref, wind_ref, vert_ref, row_ref, col_ref, out_ref,
-    inb, x, xb, kap, wbuf, fb, mf, me, ze, zf, g, rb, zb, ob,
-    in_sem, dif_sem, out_sem, loc_e, loc_y,
-    halo_s, halo_r, kap_s, kap_r, raw_s, raw_r, f_s, f_r, e_s, e_r, y_s, y_r, go_sem,
+    inb, x, xb, kap, wbuf, fb, mf, me, md, ze, zf, g, rb, zb, ob,
+    in_sem, dif_sem, out_sem, loc_e, loc_y, loc_d,
+    halo_s, halo_r, kap_s, kap_r, raw_s, raw_r, f_s, f_r, e_s, e_r, y_s, y_r, d_s, d_r, go_sem,
 ):
     w = lax.axis_index("win")
     tile = lax.axis_index("tile")
@@ -60,10 +62,20 @@
 
     pl.when(has_prev)(lambda: greet((w, tile - 1)))
     pl.when(has_next)(lambda: greet((w, tile + 1)))
-    for d in range(1, 4):
-        greet((w, lax.rem(a + d, 4) * 8 + yy))
-    for d in range(1, 8):
-        greet((w, a * 8 + lax.rem(yy + d, 8)))
+
+    @pl.when(even)
+    def _():
+        @pl.loop(1, 32)
+        def _(d):
+            greet((w, lax.rem(tile + d, 32)))
+
+    @pl.when(odd)
+    def _():
+        for d in range(1, 4):
+            greet((w, lax.rem(a + d, 4) * 8 + yy))
+        for d in range(1, 8):
+            greet((w, a * 8 + lax.rem(yy + d, 8)))
+
     sib = w + 1 - 2 * core
     greet((sib, tile))
 
@@ -103,23 +115,72 @@
     for cp in dif_cps:
         cp.wait()
 
-    peers = 11 + has_prev.astype(jnp.int32) + has_next.astype(jnp.int32) + jnp.where(sends_f, 4, 0)
+    def level_mix(fields, c, dst, scale=None, base=None):
+        @pl.loop(0, ROWS // 2)
+        def _(pair):
+            parts = []
+            for i in range(2):
+                y = 2 * pair + i
+                v = fields[c, H + y, PAD : PAD + L, :]
+                if scale is not None:
+                    v = v * scale
+                if base is not None:
+                    v = v - base[c, pl.ds(y, L, stride=8), :]
+                parts.append(v)
+            hi, lo = split2(jnp.concatenate(parts, axis=1))
+            mixed = jnp.dot(vv, jnp.concatenate([hi, lo], axis=0), preferred_element_type=F32)
+            for i in range(2):
+                if dst is md:
+                    at = pl.ds(pl.multiple_of(8 * pair, 8) + 4 * i, 4)
+                    for t in range(32):
+                        dst[t, c, at, :] = mixed[4 * t : 4 * t + 4, 128 * i : 128 * i + 128]
+                    continue
+                for b in range(4):
+                    dst[b, c, 2 * pair + i] = mixed[32 * b : 32 * b + 32, 128 * i : 128 * i + 128]
+
+    @pl.when(sends_f)
+    def _():
+        for c in range(C):
+            level_mix(x, c, mf)
+
+    peers = jnp.where(even, 32, 11) + has_prev.astype(jnp.int32) + has_next.astype(jnp.int32) + jnp.where(sends_f, 4, 0)
     pl.semaphore_wait(bar, peers)
+
+    def remote(src, dst, ss, rs, dev):
+        return pltpu.make_async_remote_copy(
+            src_ref=src, dst_ref=dst, send_sem=ss, recv_sem=rs, device_id=dev, device_id_type=MESH
+        )
 
     raw = pltpu.make_async_remote_copy(
         src_ref=inb, dst_ref=fb, send_sem=raw_s, recv_sem=raw_r,
         device_id=(sib, tile), device_id_type=MESH,
     )
 
-    @pl.when(odd)
-    def _():
-        raw.start()
+    pl.when(odd)(lambda: raw.start())
+
+    f_cps = [
+        [
+            remote(
+                mf.at[lax.rem(a + d, 4), c], zf.at[a, c], f_s.at[c, d], f_r.at[c, d],
+                (lax.rem(w + 15, 16), lax.rem(a + d, 4) * 8 + yy),
+            )
+            for d in range(4)
+        ]
+        for c in range(C)
+    ]
+
+    edge = jnp.logical_or(yy == 0, yy == 7)
+
+    @pl.when(jnp.logical_and(sends_f, jnp.logical_not(edge)))
+    def _():
+        for cps in f_cps:
+            for cp in cps:
+                cp.start()
+
+    @pl.when(even)
+    def _():
         pl.semaphore_wait(go_sem, 1)
 
-    def remote(src, dst, ss, rs, dev):
-        return pltpu.make_async_remote_copy(
-            src_ref=src, dst_ref=dst, send_sem=ss, recv_sem=rs, device_id=dev, device_id_type=MESH
-        )
 
     zs = pl.ds(PAD, L)
     up = remote(
@@ -133,6 +194,12 @@
     kup = remote(kap.at[1], kap.at[2], kap_s.at[0], kap_r.at[0], (w, tile - 1))
     kdown = remote(kap.at[1], kap.at[0], kap_s.at[1], kap_r.at[1], (w, tile + 1))
 
+    @pl.when(jnp.logical_and(sends_f, edge))
+    def _():
+        for cps in f_cps:
+            for cp in cps:
+                cp.start()
+
     @pl.when(has_prev)
     def _():
         kup.start()
@@ -143,50 +210,13 @@
         kdown.start()
         down.start()
 
-    def level_mix(fields, c, dst, scale=None, base=None):
-        @pl.loop(0, ROWS // 2)
-        def _(pair):
-            parts = []
-            for i in range(2):
-                y = 2 * pair + i
-                v = fields[c, H + y, PAD : PAD + L, :]
-                if scale is not None:
-                    v = v * scale - base[c, pl.ds(y, L, stride=8), :]
-                parts.append(v)
-            hi, lo = split2(jnp.concatenate(parts, axis=1))
-            mixed = jnp.dot(vv, jnp.concatenate([hi, lo], axis=0), preferred_element_type=F32)
-            for i in range(2):
-                for b in range(4):
-                    dst[b, c, 2 * pair + i] = mixed[32 * b : 32 * b + 32, 128 * i : 128 * i + 128]
-
-    f_cps = [
-        remote(
-            mf.at[lax.rem(a + d, 4)], zf.at[a], f_s.at[d], f_r.at[d],
-            (lax.rem(w + 15, 16), lax.rem(a + d, 4) * 8 + yy),
-        )
-        for d in range(4)
-    ]
-
-    @pl.when(sends_f)
-    def _():
-        for c in range(C):
-            level_mix(x, c, mf)
-        for cp in f_cps:
-            cp.start()
-
-    @pl.when(jnp.logical_not(gets_f))
+    @pl.when(w == 15)
     def _():
         @pl.loop(0, 4)
         def _(i):
             for c in range(C):
                 zf[i, c] = jnp.zeros((ROWS, 32, 128), F32)
 
-    @pl.when(odd)
-    def _():
-        @pl.loop(0, C)
-        def _(c):
-            fb[c] = jnp.zeros((L * ROWS, 128), F32)
-
     @pl.when(has_prev)
     def _():
         kup.wait_send()
@@ -199,7 +229,7 @@
         kup.wait_recv()
         up.wait_recv()
 
-    @pl.when(even)
+    @pl.when(jnp.logical_not(even))
     def _():
         pl.semaphore_signal(go_sem, inc=1, device_id=(sib, tile), device_id_type=MESH)
 
@@ -241,35 +271,51 @@
         step(2 * h, x, xb)
         step(2 * h + 1, xb, x)
 
-    pl.when(even)(lambda: raw.wait_recv())
+    d_cps = {}
+    for d in ORDER:
+        dz, dy = d // 8, d % 8
+        t = lax.rem(a + dz, 4) * 8 + lax.rem(yy + dy, 8)
+        d_cps[d] = remote(
+            md.at[t], rb.at[yy, :, pl.ds(pl.multiple_of(32 * a, 32), 32)], d_s.at[d], d_r.at[d], (w, t)
+        )
+    d_loc = pltpu.make_async_copy(md.at[tile], rb.at[yy, :, pl.ds(pl.multiple_of(32 * a, 32), 32)], loc_d)
+
+    @pl.when(even)
+    def _():
+        raw.wait_recv()
+        for c in range(C):
+            level_mix(x, c, md, 1e-6, fb)
+        for d in ORDER:
+            d_cps[d].start()
+        d_loc.start()
+        d_loc.wait()
 
     e_cps = [[None] * 4 for _ in range(C)]
     e_loc = []
-    for c in range(C):
-        level_mix(x, c, me, 1e-6, fb)
-        for d in (1, 3, 2):
-            b = lax.rem(a + d, 4)
-            cp = remote(me.at[b, c], ze.at[a, c], e_s.at[c, d], e_r.at[c, d], (w, b * 8 + yy))
-            cp.start()
-            e_cps[c][d] = cp
-        cp = pltpu.make_async_copy(me.at[a, c], ze.at[a, c], loc_e.at[c])
-        cp.start()
-        e_loc.append(cp)
-
-    @pl.when(gets_f)
-    def _():
-        for cp in f_cps:
-            cp.wait_recv()
-
     y_cps = [[None] * 8 for _ in range(C)]
     y_loc = []
     for c in range(C):
         for d in (1, 3, 2):
-            e_cps[c][d].wait_recv()
-        e_loc[c].wait()
-
+            b = lax.rem(a + d, 4)
+            e_cps[c][d] = remote(me.at[b, c], ze.at[a, c], e_s.at[c, d], e_r.at[c, d], (w, b * 8 + yy))
+        e_loc.append(pltpu.make_async_copy(me.at[a, c], ze.at[a, c], loc_e.at[c]))
+        for d in (1, 7, 2, 6, 3, 5, 4):
+            t = lax.rem(yy + d, 8)
+            y_cps[c][d] = remote(g.at[c, t], rb.at[yy, c], y_s.at[c, d], y_r.at[c, d], (w, a * 8 + t))
+        y_loc.append(pltpu.make_async_copy(g.at[c, yy], rb.at[yy, c], loc_y.at[c]))
+
+    def send_levels(c):
+        level_mix(x, c, me, 1e-6)
+        if c >= AHEAD:
+            for d in (1, 3, 2):
+                e_cps[c - AHEAD][d].wait_recv()
+        for d in (1, 3, 2):
+            e_cps[c][d].start()
+        e_loc[c].start()
+
+    def send_rows(c):
         @pl.loop(0, 4)
-        def _(i, c=c):
+        def _(i):
             for y in range(ROWS):
                 for t in range(4):
                     v = ze[i, c, y, 8 * t : 8 * t + 8, :] - zf[i, c, y, 8 * t : 8 * t + 8, :]
@@ -277,22 +323,47 @@
                     g[c, 2 * t, at, :] = v[0:4]
                     g[c, 2 * t + 1, at, :] = v[4:8]
 
-        for d in (1, 7, 2, 6, 3, 5, 4):
-            t = lax.rem(yy + d, 8)
-            cp = remote(g.at[c, t], rb.at[yy, c], y_s.at[c, d], y_r.at[c, d], (w, a * 8 + t))
-            cp.start()
-            y_cps[c][d] = cp
-        cp = pltpu.make_async_copy(g.at[c, yy], rb.at[yy, c], loc_y.at[c])
-        cp.start()
-        y_loc.append(cp)
-
-    for d in (0, 1, 7, 2, 6, 3, 5, 4):
+        for d in (4, 3, 5, 2, 6, 1, 7):
+            y_cps[c][d].start()
+        y_loc[c].start()
+
+    @pl.when(odd)
+    def _():
+        for c in range(AHEAD):
+            send_levels(c)
+        for c in range(C):
+            if c + AHEAD < C:
+                send_levels(c + AHEAD)
+            else:
+                for d in (1, 3, 2):
+                    e_cps[c][d].wait_recv()
+            e_loc[c].wait()
+
+            @pl.when(gets_f)
+            def _(c=c):
+                for cp in f_cps[c]:
+                    cp.wait_recv()
+
+            send_rows(c)
+        for c in range(C):
+            y_loc[c].wait()
+
+    for d in (0, 4, 3, 5, 2, 6, 1, 7):
         src = lax.rem(yy + 8 - d, 8)
-        for c in range(C):
-            if d == 0:
-                y_loc[c].wait()
-            else:
-                y_cps[c][d].wait_recv()
+
+        @pl.when(even)
+        def _(d=d):
+            for dz in range(4):
+                if dz or d:
+                    d_cps[dz * 8 + d].wait_recv()
+
+        if d:
+
+            @pl.when(odd)
+            def _(d=d):
+                for c in range(C):
+                    y_cps[c][d].wait_recv()
+
         total = None
         for c in range(C):
             v = jnp.concatenate([rb[src, c, pl.ds(z, 32, stride=4), :] for z in range(4)], axis=0)
@@ -318,14 +389,23 @@
 
     @pl.when(sends_f)
     def _():
-        for cp in f_cps:
-            cp.wait_send()
-
-    for c in range(C):
-        for d in range(1, 4):
-            e_cps[c][d].wait_send()
-        for d in range(1, 8):
-            y_cps[c][d].wait_send()
+        for cps in f_cps:
+            for cp in cps:
+                cp.wait_send()
+
+    @pl.when(even)
+    def _():
+        for d in ORDER:
+            d_cps[d].wait_send()
+
+    @pl.when(odd)
+    def _():
+        for c in range(C):
+            for d in range(1, 4):
+                e_cps[c][d].wait_send()
+            for d in range(1, 8):
+                y_cps[c][d].wait_send()
+
     for cp in outs:
         cp.wait()
 
@@ -348,15 +428,16 @@
             pltpu.VMEM((C, L * ROWS, 128), F32),
             pltpu.VMEM((4, C, ROWS, 32, 128), F32),
             pltpu.VMEM((4, C, ROWS, 32, 128), F32),
+            pltpu.VMEM((32, C, 32, 128), F32),
             pltpu.VMEM((4, C, ROWS, 32, 128), F32),
             pltpu.VMEM((4, C, ROWS, 32, 128), F32),
             pltpu.VMEM((C, 8, 128, 128), F32),
             pltpu.VMEM((8, C, 128, 128), F32),
             pltpu.VMEM((4, NY, NX), F32),
             pltpu.VMEM((4, NY, NX), F32),
-            dma((C,)), dma((C,)), dma((4,)), dma((C,)), dma((C,)),
+            dma((C,)), dma((C,)), dma((4,)), dma((C,)), dma((C,)), dma,
             dma((2,)), dma((2,)), dma((2,)), dma((2,)), dma, dma,
-            dma((4,)), dma((4,)), dma((C, 4)), dma((C, 4)), dma((C, 8)), dma((C, 8)),
+            dma((C, 4)), dma((C, 4)), dma((C, 4)), dma((C, 4)), dma((C, 8)), dma((C, 8)), dma((32,)), dma((32,)),
             pltpu.SemaphoreType.REGULAR,
         ],
         compiler_params=pltpu.CompilerParams(

time: 143 us -> 129 us (0.902)
  the two profiles are of different devices: /device:TPU:399 before, /device:TPU:27 now
where the time goes in v2:
time: 129 us
  Pallas kernels  126 us (98%)
  local copies, waits for them, and re-layouts  3.08 us (2%)
    pallas_call x1, Pallas kernels, body(): pl.pallas_call(kernel, out_shape=jax.ShapeDtypeStruct((4, NY, NX), F32),...  126 us
    unnamed x1, local copies, waits for them, and re-layouts  3.08 us

profile of v2, /device:TPU:27, one launch (start us, length us, event | category | flops | bytes accessed | tf_op | source)
XLA Modules:
  0.0 129.2 jit_solution(5598016058839244582)
XLA Ops:
  0.0 126.1 %shard_map.64 = f32[4,256,512]{2,1,0:T(8,128)} custom-call(f32[1024,512]{1,0:T(8,128)} %bitcast.4, f32[8,512]{1,0:T(8,128)} %bitcast.5, f32[1,128]{1,0:T(1,128)} %wind_ref.1, bf16[128,128]{1,0:T(8,128)(2,1)} %vert_ref.1, bf16[256,256]{1,0:T(8,128)(2,1)} %row_ref.1, bf16[512,512]{1,0:T(8,128)(2,1)} %col_ref.1), custom_call_target="tpu_custom_call" | custom-call | tf_op jit(solution)/shard_map/pallas_call | solution.py:417
  126.1 3.1 %copy.8 = f32[1,4,256,512]{3,2,1,0:T(8,128)} copy(f32[1,4,256,512]{3,2,1,0:T(8,128)} %bitcast.3) | data formatting | bytes 4194304

commit v3 on v2

--- a/solution.py
+++ b/solution.py
@@ -28,9 +28,9 @@
 
 def kernel(
     inc_ref, dif_ref, wind_ref, vert_ref, row_ref, col_ref, out_ref,
-    inb, x, xb, kap, wbuf, fb, mf, me, md, ze, zf, g, rb, zb, ob,
+    inb, x, xb, rel, kap, wbuf, fb, mf, me, md, ze, zf, g, rb, zb, ob,
     in_sem, dif_sem, out_sem, loc_e, loc_y, loc_d,
-    halo_s, halo_r, kap_s, kap_r, raw_s, raw_r, f_s, f_r, e_s, e_r, y_s, y_r, d_s, d_r, go_sem,
+    halo_s, halo_r, rel_s, rel_r, kap_s, kap_r, raw_s, raw_r, f_s, f_r, e_s, e_r, y_s, y_r, d_s, d_r, go_sem,
 ):
     w = lax.axis_index("win")
     tile = lax.axis_index("tile")
@@ -169,46 +169,62 @@
         for c in range(C)
     ]
 
-    edge = jnp.logical_or(yy == 0, yy == 7)
-
-    @pl.when(jnp.logical_and(sends_f, jnp.logical_not(edge)))
+    @pl.when(sends_f)
     def _():
         for cps in f_cps:
             for cp in cps:
                 cp.start()
 
-    @pl.when(even)
-    def _():
-        pl.semaphore_wait(go_sem, 1)
-
 
     zs = pl.ds(PAD, L)
-    up = remote(
-        x.at[:, pl.ds(H, H), zs], x.at[:, pl.ds(H + ROWS, H), zs],
-        halo_s.at[0], halo_r.at[0], (w, tile - 1),
-    )
-    down = remote(
-        x.at[:, pl.ds(ROWS, H), zs], x.at[:, pl.ds(0, H), zs],
-        halo_s.at[1], halo_r.at[1], (w, tile + 1),
-    )
+    def starts(cps):
+        for cp in cps:
+            cp.start()
+
+    parts = ((0, 2), (2, 1), (3, 1))
+
+    def halo(way, part, dev, via=None):
+        first = (H, ROWS)[way]
+        cs = pl.ds(*parts[part])
+        return remote(
+            x.at[cs, pl.ds(first, H), zs],
+            x.at[cs, pl.ds((H + ROWS, 0)[way], H), zs] if via is None else rel.at[pl.ds(part - 1, 1)],
+            halo_s.at[way, part], halo_r.at[way, part] if via is None else rel_r.at[part - 1],
+            (w, dev if via is None else via),
+        )
+
+    ups = [halo(0, n, tile - 1) for n in range(3)]
+    downs = [halo(1, n, tile + 1) for n in range(3)]
+    ups_via = [halo(0, n, None, tile - 8) for n in (1, 2)]
+    downs_via = [halo(1, n, None, tile + 8) for n in (1, 2)]
+    at_start, at_end = yy == 0, yy == 7
+
+    def passed(way, part, dev):
+        return remote(
+            rel.at[pl.ds(part - 1, 1)], x.at[pl.ds(*parts[part]), pl.ds((H + ROWS, 0)[way], H), zs],
+            rel_s.at[part - 1], halo_r.at[way, part], (w, dev),
+        )
+
+    pass_up = [passed(0, n, tile + 7) for n in (1, 2)]
+    pass_down = [passed(1, n, tile - 7) for n in (1, 2)]
+    passes_up = jnp.logical_and(at_start, a < 3)
+    passes_down = jnp.logical_and(at_end, a > 0)
     kup = remote(kap.at[1], kap.at[2], kap_s.at[0], kap_r.at[0], (w, tile - 1))
     kdown = remote(kap.at[1], kap.at[0], kap_s.at[1], kap_r.at[1], (w, tile + 1))
 
-    @pl.when(jnp.logical_and(sends_f, edge))
-    def _():
-        for cps in f_cps:
-            for cp in cps:
-                cp.start()
-
     @pl.when(has_prev)
     def _():
         kup.start()
-        up.start()
+        pl.when(at_start)(lambda: starts(ups_via))
+        pl.when(jnp.logical_not(at_start))(lambda: starts(ups[1:]))
+        ups[0].start()
 
     @pl.when(has_next)
     def _():
         kdown.start()
-        down.start()
+        pl.when(at_end)(lambda: starts(downs_via))
+        pl.when(jnp.logical_not(at_end))(lambda: starts(downs[1:]))
+        downs[0].start()
 
     @pl.when(w == 15)
     def _():
@@ -217,24 +233,42 @@
             for c in range(C):
                 zf[i, c] = jnp.zeros((ROWS, 32, 128), F32)
 
+    @pl.when(passes_up)
+    def _():
+        for got, on in zip(ups_via, pass_up):
+            got.wait_recv()
+            on.start()
+
+    @pl.when(passes_down)
+    def _():
+        for got, on in zip(downs_via, pass_down):
+            got.wait_recv()
+            on.start()
+
     @pl.when(has_prev)
     def _():
         kup.wait_send()
         kdown.wait_recv()
-        down.wait_recv()
+        for cp in downs:
+            cp.wait_recv()
 
     @pl.when(has_next)
     def _():
         kdown.wait_send()
         kup.wait_recv()
-        up.wait_recv()
-
-    @pl.when(jnp.logical_not(even))
-    def _():
-        pl.semaphore_signal(go_sem, inc=1, device_id=(sib, tile), device_id_type=MESH)
-
-    pl.when(has_prev)(lambda: up.wait_send())
-    pl.when(has_next)(lambda: down.wait_send())
+        for cp in ups:
+            cp.wait_recv()
+
+    @pl.when(has_prev)
+    def _():
+        for cp in ups:
+            cp.wait_send()
+
+    @pl.when(has_next)
+    def _():
+        for cp in downs:
+            cp.wait_send()
+
 
     lane = lax.broadcasted_iota(jnp.int32, (8, 128), 1)
     first_lane, last_lane = lane == 0, lane == 127
@@ -406,6 +440,16 @@
             for d in range(1, 8):
                 y_cps[c][d].wait_send()
 
+    @pl.when(passes_up)
+    def _():
+        for cp in pass_up:
+            cp.wait_send()
+
+    @pl.when(passes_down)
+    def _():
+        for cp in pass_down:
+            cp.wait_send()
+
     for cp in outs:
         cp.wait()
 
@@ -423,6 +467,7 @@
             pltpu.VMEM((C, L * ROWS, 128), F32),
             pltpu.VMEM((C, R20, L + 2 * PAD, 128), F32),
             pltpu.VMEM((C, R20, L + 2 * PAD, 128), F32),
+            pltpu.VMEM((C // 2, H, L, 128), F32),
             pltpu.VMEM((3, C, ROWS, 128), F32),
             pltpu.VMEM((L, 128), F32),
             pltpu.VMEM((C, L * ROWS, 128), F32),
@@ -436,7 +481,7 @@
             pltpu.VMEM((4, NY, NX), F32),
             pltpu.VMEM((4, NY, NX), F32),
             dma((C,)), dma((C,)), dma((4,)), dma((C,)), dma((C,)), dma,
-            dma((2,)), dma((2,)), dma((2,)), dma((2,)), dma, dma,
+            dma((2, 3)), dma((2, 3)), dma((2,)), dma((2,)), dma((2,)), dma((2,)), dma, dma,
             dma((C, 4)), dma((C, 4)), dma((C, 4)), dma((C, 4)), dma((C, 8)), dma((C, 8)), dma((32,)), dma((32,)),
             pltpu.SemaphoreType.REGULAR,
         ],

time: 129 us -> 127 us (0.984)
  the two profiles are of different devices: /device:TPU:27 before, /device:TPU:1 now
where the time goes in v3:
time: 127 us
  Pallas kernels  124 us (98%)
  local copies, waits for them, and re-layouts  3.08 us (2%)
    pallas_call x1, Pallas kernels, body(): pl.pallas_call(kernel, out_shape=jax.ShapeDtypeStruct((4, NY, NX), F32),...  124 us
    unnamed x1, local copies, waits for them, and re-layouts  3.08 us

profile of v3, /device:TPU:1, one launch (start us, length us, event | category | flops | bytes accessed | tf_op | source)
XLA Modules:
  0.0 126.7 jit_solution(15682149551623485306)
XLA Ops:
  0.0 123.6 %shard_map.64 = f32[4,256,512]{2,1,0:T(8,128)} custom-call(f32[1024,512]{1,0:T(8,128)} %bitcast.4, f32[8,512]{1,0:T(8,128)} %bitcast.5, f32[1,128]{1,0:T(1,128)} %wind_ref.1, bf16[128,128]{1,0:T(8,128)(2,1)} %vert_ref.1, bf16[256,256]{1,0:T(8,128)(2,1)} %row_ref.1, bf16[512,512]{1,0:T(8,128)(2,1)} %col_ref.1), custom_call_target="tpu_custom_call" | custom-call | tf_op jit(solution)/shard_map/pallas_call | solution.py:461
  123.6 3.1 %copy.8 = f32[1,4,256,512]{3,2,1,0:T(8,128)} copy(f32[1,4,256,512]{3,2,1,0:T(8,128)} %bitcast.3) | data formatting | bytes 4194304
